TPU v7x, 128 devices: a whole 4x4x4 slice. The times are simulated.
128 devices in a mesh: dp: 4 (over y), owner: 32 (over x, z, core).
Axes of the slice: x: 4, y: 4, z: 4, core: 2. Of those that a mesh axis runs over, the one named last changes fastest.
Arguments:
- gradient: bfloat16 [128, 2048, 768], P(None, ('dp', 'owner'))
- momentum: float32 [128, 2048, 768], P(None, ('dp', 'owner'))
- owner_table: int32 [128], replicated, may hold values from 0 to 127, as said below
Outputs:
- new_momentum: float32 [128, 2048, 768], P(None, ('dp', 'owner'))
- update: bfloat16 [128, 2048, 768], P(None, ('dp', 'owner'))
- owner_log: float32 [128, 2], P(('dp', 'owner'))
Inputs may be any that keep to these rules, and one draw needn't show every extreme that they name: `owner_table`: each device owns at most 2 matrices; in every draw some device owns exactly 2.
All inputs are finite; a program needn't handle non-finite values.
Results may differ from a plain program's by a relative error of at most 0.0076.
Values may be sent and summed in bfloat16 or wider, within the bound.
A program may use at most 128 MiB of HBM per device.

v0:
```python
import math

import jax
import jax.numpy as jnp
from jax import lax
from jax.sharding import PartitionSpec as P

CAP = 2
NS_STEPS = 2


momentum_decay = 0.95
linear_coef = 3.4445
cubic_coef = -4.775
quintic_coef = 2.0315
norm_epsilon = 1e-07


def orthogonalize(matrices_in):
    current = matrices_in
    for repeat in range(NS_STEPS):
        current = lax.optimization_barrier(current)
        gram_mat = jnp.einsum(
            "sdf,sdg->sfg", current, current, preferred_element_type=jnp.float32
        ).astype(jnp.bfloat16)
        gram_mat = lax.optimization_barrier(gram_mat)
        square = jnp.einsum("sfg,sgh->sfh", gram_mat, gram_mat, preferred_element_type=jnp.float32)
        poly_mat = (cubic_coef * gram_mat.astype(jnp.float32) + quintic_coef * square).astype(
            jnp.bfloat16
        )
        current = (
            linear_coef * current.astype(jnp.float32)
            + jnp.einsum("sdf,sfg->sdg", current, poly_mat, preferred_element_type=jnp.float32)
        ).astype(jnp.bfloat16)
    return current


def route_rows(buffer):
    return lax.all_to_all(buffer, ("dp", "owner"), split_axis=1, concat_axis=1, tiled=True)


def on_device(gradient, momentum, owner_table):
    matrices, row_count, col_count = gradient.shape
    device_count = lax.axis_size(("dp", "owner"))
    full_rows = row_count * device_count
    grad_float = gradient.astype(jnp.float32)
    fresh = momentum_decay * momentum + grad_float
    rounded = lax.optimization_barrier((grad_float + momentum_decay * fresh).astype(jnp.bfloat16))
    rounded_float = rounded.astype(jnp.float32)
    partial_value = jnp.sum(rounded_float * rounded_float, axis=(1, 2))
    totals = lax.psum(partial_value, ("dp", "owner"))
    payload = (rounded_float / (jnp.sqrt(totals) + norm_epsilon)[:, None, None]).astype(
        jnp.bfloat16
    )
    position = jnp.arange(matrices, dtype=jnp.int32)
    same_owner = owner_table[:, None] == owner_table[None, :]
    earlier_one = position[None, :] < position[:, None]
    slot_rank = jnp.sum((same_owner & earlier_one).astype(jnp.int32), axis=1)
    target = slot_rank * device_count + owner_table
    buffer = (
        jnp.zeros((CAP * device_count, row_count, col_count), jnp.bfloat16).at[target].set(payload)
    )
    received = route_rows(buffer.reshape(CAP, device_count, row_count, col_count))
    orthogonal = orthogonalize(received.reshape(CAP, full_rows, col_count))
    ortho_float = orthogonal.astype(jnp.float32)
    rms_slots = math.sqrt(full_rows) * jnp.sqrt(
        jnp.sum(ortho_float * ortho_float, axis=(1, 2)) / (full_rows * col_count)
    )
    owner_log = rms_slots[None, :]
    returned = route_rows(orthogonal.reshape(CAP, device_count, row_count, col_count))
    gathered_rows = returned.reshape(CAP * device_count, row_count, col_count)[target]
    update = (math.sqrt(full_rows) * gathered_rows.astype(jnp.float32)).astype(jnp.bfloat16)
    return (fresh, update, owner_log)


def solution(mesh):
    return jax.shard_map(
        on_device,
        mesh=mesh,
        in_specs=(P(None, ("dp", "owner"), None), P(None, ("dp", "owner"), None), P()),
        out_specs=(
            P(None, ("dp", "owner"), None),
            P(None, ("dp", "owner"), None),
            P(("dp", "owner"), None),
        ),
        check_vma=False,
    )
```

profile of v0, /device:TPU:1, one launch (start us, length us, event | category | flops | bytes accessed | tf_op | source)
XLA Modules:
  0.0 332.3 jit_solution(16739914786121134504)
XLA Ops:
  0.6 0.9 convert_reduce_fusion
  1.5 0.7 compare_select_fusion
  2.2 7.8 %fusion = (bf16[128,16,768]{2,1,0:T(8,128)(2,1)S(1)}, f32[128,16,768]{2,1,0:T(8,128)}) fusion(bf16[128,16,768]{2,1,0:T(8,128)(2,1)} %param.3, f32[128,16,768]{2,1,0:T(8,128)} %param.4), kind=kLoop, calls=%fused_computation.9 | loop fusion | flops 9437184 | bytes 18874368 | tf_op jit(solution)/shard_map/convert_element_type | solution.py:48
  10.0 1.0 fusion.1
  11.1 68.7 %psum.7 = f32[128]{0:T(128)S(1)} all-reduce(f32[128]{0:T(128)S(1)} %fusion.1), channel_id=1, replica_groups=mesh['dp'=4,'owner'=32] {'dp','owner'}, use_global_device_ids=true, to_apply=%region_2.0 | all-reduce | flops 128 | bytes 1024 | tf_op jit(solution)/shard_map/psum | solution.py:51
  79.8 2.7 fusion.2
  82.5 0.0 copy-start
  82.5 3.1 broadcast_in_dim.4
  85.6 0.1 copy-done
  85.7 16.3 %scatter_fusion = bf16[256,16,768]{2,1,0:T(8,128)(2,1)} fusion(bf16[256,16,768]{2,1,0:T(8,128)(2,1)} %broadcast_in_dim.4, s32[128]{0:T(128)S(1)} %compare_select_fusion, bf16[128,16,768]{2,1,0:T(8,128)(2,1)S(1)} %copy-done), kind=kCustom, calls=%fused_computation.1 | custom fusion | bytes 9437696 | tf_op jit(solution)/shard_map/scatter | solution.py:61
  101.9 3.7 %copy.16 = bf16[2,128,16,768]{3,2,0,1:T(8,128)(2,1)S(1)} copy(bf16[2,128,16,768]{3,2,1,0:T(8,128)(2,1)} %bitcast.16) | data formatting | bytes 12582912 | tf_op jit(solution)/shard_map/reshape | solution.py:63
  105.7 79.7 %all_to_all.10 = bf16[2,128,16,768]{3,2,0,1:T(8,128)(2,1)S(1)} all-to-all(bf16[2,128,16,768]{3,2,0,1:T(8,128)(2,1)S(1)} %copy.16), channel_id=1, replica_groups=mesh['dp'=4,'owner'=32] {'dp','owner'}, dimensions={1} | all-to-all | bytes 12582912 | tf_op jit(solution)/shard_map/all_to_all | solution.py:39
  185.3 0.5 copy.17
  185.8 0.0 copy-start.1
  185.9 2.6 copy-done.1
  188.5 5.7 %convolution_convert_fusion.1 = bf16[2,768,768]{2,1,0:T(8,128)(2,1)S(1)} fusion(bf16[2,2048,768]{2,1,0:T(8,128)(2,1)S(1)} %bitcast.19), kind=kOutput, calls=%fused_computation.20 | convolution fusion | flops 4833017856 | bytes 8650752 | tf_op jit(solution)/shard_map/sdf,sdg->sfg/dot_general | solution.py:23
  194.2 13.5 %add_convert_fusion.1 = bf16[2,2048,768]{2,1,0:T(8,128)(2,1)} fusion(bf16[2,2048,768]{2,1,0:T(8,128)(2,1)} %bitcast.20, bf16[2,768,768]{2,1,0:T(8,128)(2,1)S(1)} %convolution_convert_fusion.1), kind=kOutput, calls=%fused_computation.4 | convolution fusion | flops 6662258688 | bytes 14942208 | tf_op jit(solution)/shard_map/sdf,sfg->sdg/dot_general | solution.py:33
  207.7 9.1 %convolution_convert_fusion = bf16[2,768,768]{2,1,0:T(8,128)(2,1)S(1)} fusion(bf16[2,2048,768]{2,1,0:T(8,128)(2,1)} %add_convert_fusion.1), kind=kOutput, calls=%fused_computation.19 | convolution fusion | flops 4833017856 | bytes 8650752 | tf_op jit(solution)/shard_map/sdf,sdg->sfg/dot_general | solution.py:23
  216.8 14.6 %multiply_reduce_fusion = (f32[2]{0:T(128)S(1)}, bf16[2,2048,768]{2,1,0:T(8,128)(2,1)}) fusion(bf16[2,2048,768]{2,1,0:T(8,128)(2,1)} %add_convert_fusion.1, bf16[2,768,768]{2,1,0:T(8,128)(2,1)S(1)} %convolution_convert_fusion), kind=kOutput, calls=%fused_computation.2 | convolution fusion | flops 6671695872 | bytes 14942216 | tf_op jit(solution)/shard_map/sdf,sfg->sdg/dot_general | solution.py:33
  231.4 6.4 %copy.20 = bf16[2,128,16,768]{3,2,0,1:T(8,128)(2,1)} copy(bf16[2,128,16,768]{3,2,1,0:T(8,128)(2,1)} %bitcast.18) | data formatting | bytes 12582912 | tf_op jit(solution)/shard_map/reshape | solution.py:70
  237.7 5.8 %all-to-all-start.1 = ((bf16[2,128,16,768]{3,2,0,1:T(8,128)(2,1)}), bf16[2,128,16,768]{3,2,0,1:T(8,128)(2,1)}, u32[]{:S(2)}, u32[]{:S(2)}) async-start(bf16[2,128,16,768]{3,2,0,1:T(8,128)(2,1)} %copy.20), calls=%async_computation.1 | async-start | bytes 12582912 | tf_op jit(solution)/shard_map/all_to_all | solution.py:39
  243.6 0.5 multiply_bitcast_fusion
  244.1 76.4 %all-to-all-done.1 = bf16[2,128,16,768]{3,2,0,1:T(8,128)(2,1)} async-done(((bf16[2,128,16,768]{3,2,0,1:T(8,128)(2,1)}), bf16[2,128,16,768]{3,2,0,1:T(8,128)(2,1)}, u32[]{:S(2)}, u32[]{:S(2)}) %all-to-all-start.1) | async-done | bytes 6291488 | tf_op jit(solution)/shard_map/all_to_all | solution.py:39
  320.5 5.9 %copy.21 = bf16[2,128,16,768]{3,2,1,0:T(8,128)(2,1)} copy(bf16[2,128,16,768]{3,2,0,1:T(8,128)(2,1)} %all-to-all-done.1) | data formatting | bytes 12582912 | tf_op jit(solution)/shard_map/all_to_all | solution.py:39
  326.5 3.5 %gather_fusion = bf16[128,16,768]{2,1,0:T(8,128)(2,1)S(1)} fusion(bf16[256,16,768]{2,1,0:T(8,128)(2,1)} %bitcast.17, s32[1024]{0:T(1024)S(1)} %pad_clamp_fusion), kind=kCustom, calls=%fused_computation | custom fusion | bytes 6291968 | tf_op jit(solution)/shard_map/gather | solution.py:71
  330.0 2.3 multiply_convert_fusion
  (2 shorter events, 0.0 us)
Async XLA Ops:
  82.5 3.2 copy-start
  185.8 2.7 copy-start.1
  237.7 82.8 %all-to-all-start.1 = ((bf16[2,128,16,768]{3,2,0,1:T(8,128)(2,1)}), bf16[2,128,16,768]{3,2,0,1:T(8,128)(2,1)}, u32[]{:S(2)}, u32[]{:S(2)}) async-start(bf16[2,128,16,768]{3,2,0,1:T(8,128)(2,1)} %copy.20), calls=%async_computation.1 | async-start | bytes 12582912 | tf_op jit(solution)/shard_map/all_to_all | solution.py:39
where the time goes:
time: 333 us; the launch traced here: 332 us
  blocking collectives  148 us (44%)
  waiting for transfers between devices  76.4 us (23%)
  matrix products  42.8 us (13%)
  local copies, waits for them, and re-layouts  42.2 us (13%)
  other arithmetic  16 us (5%)
  starting transfers between devices  5.81 us (2%)
    all_to_all x1, blocking collectives, route_rows(): lax.all_to_all(buffer, ('dp', 'owner'), split_axis=1, concat_axis=1, tile...  79.7 us
    all_to_all x1, waiting for transfers between devices, route_rows(): lax.all_to_all(buffer, ('dp', 'owner'), split_axis=1, concat_axis=1, tile...  76.4 us
    psum x1, blocking collectives, on_device(): totals = lax.psum(partial_value, ('dp', 'owner'))  68.7 us
    dot_general x2, matrix products, orthogonalize(): jnp.einsum('sdf,sfg->sdg', current, poly_mat, preferred_element_type=jnp....  28.1 us
    scatter x1, local copies, waits for them, and re-layouts, on_device(): jnp.zeros((CAP * device_count, row_count, col_count), jnp.bfloat16)  16.3 us
    dot_general x2, matrix products, orthogonalize(): jnp.einsum('sdf,sdg->sfg', current, current, preferred_element_type=jnp.f...  14.8 us
    convert_element_type x1, other arithmetic, on_device(): (grad_float + momentum_decay * fresh).astype(jnp.bfloat16)  7.83 us
  transfers between devices with their start and end apart: 1, of which 1 were waited for; matrix products, arithmetic and copies ran while one was open for 0% of the time, Pallas kernels for 0%

commit v1 on v0

v1 whole, which is shorter than its diff:
```python
import math

import jax
import jax.numpy as jnp
from jax import lax
from jax.sharding import PartitionSpec as P

CAP = 2
NS_STEPS = 2
AXES = ("dp", "owner")

momentum_decay = 0.95
linear_coef = 3.4445
cubic_coef = -4.775
quintic_coef = 2.0315
norm_epsilon = 1e-07


def orthogonalize(current):
    for repeat in range(NS_STEPS):
        gram_mat = jnp.einsum(
            "df,dg->fg", current, current, preferred_element_type=jnp.float32
        ).astype(jnp.bfloat16)
        square = jnp.dot(gram_mat, gram_mat, preferred_element_type=jnp.float32)
        poly_mat = (cubic_coef * gram_mat.astype(jnp.float32) + quintic_coef * square).astype(
            jnp.bfloat16
        )
        current = (
            linear_coef * current.astype(jnp.float32)
            + jnp.dot(current, poly_mat, preferred_element_type=jnp.float32)
        ).astype(jnp.bfloat16)
    return current


def on_device(gradient, momentum, owner_table):
    matrices, row_count, col_count = gradient.shape
    device_count = lax.axis_size(AXES)
    full_rows = row_count * device_count
    grad_float = gradient.astype(jnp.float32)
    fresh = momentum_decay * momentum + grad_float
    rounded = (grad_float + momentum_decay * fresh).astype(jnp.bfloat16)
    received = lax.all_to_all(rounded, AXES, split_axis=0, concat_axis=0, tiled=True)
    whole = received.reshape(full_rows, col_count).astype(jnp.float32)
    norm = jnp.sqrt(jnp.sum(whole * whole)) + norm_epsilon
    orthogonal = orthogonalize((whole / norm).astype(jnp.bfloat16))
    ortho_float = orthogonal.astype(jnp.float32)
    rms = math.sqrt(full_rows) * jnp.sqrt(
        jnp.sum(ortho_float * ortho_float) / (full_rows * col_count)
    )
    scaled = (math.sqrt(full_rows) * ortho_float).astype(jnp.bfloat16)
    update = lax.all_to_all(
        scaled.reshape(matrices, row_count, col_count), AXES, split_axis=0, concat_axis=0, tiled=True
    )
    every_rms = lax.all_gather(rms, AXES)
    me = lax.axis_index(AXES)
    mine = owner_table == me
    rank = jnp.cumsum(mine.astype(jnp.int32)) - 1
    slots = jnp.arange(CAP, dtype=jnp.int32)
    chosen = mine[None, :] & (rank[None, :] == slots[:, None])
    owner_log = jnp.sum(jnp.where(chosen, every_rms[None, :], 0.0), axis=1)[None, :]
    return (fresh, update, owner_log)


def solution(mesh):
    rows = P(None, AXES, None)
    return jax.shard_map(
        on_device,
        mesh=mesh,
        in_specs=(rows, rows, P()),
        out_specs=(rows, rows, P(AXES, None)),
        check_vma=False,
    )
```

time: 333 us -> 194 us (0.58)
  waiting for transfers between devices: 76.4 us -> 0.01 us
  local copies, waits for them, and re-layouts: 42.2 us -> 3.64 us
  matrix products: 42.8 us -> 26.1 us
  other arithmetic: 16 us -> 12 us
    unnamed x0 -> x1, blocking collectives: none -> 92.1 us
    all_to_all x1, waiting for transfers between devices: 76.4 us -> 0.01 us  [on_device(): lax.all_to_all(scaled.reshape(matrices, row_count, col_count), AXES, spli...]
    psum x1 -> x0, blocking collectives: 68.7 us -> none  [on_device(): totals = lax.psum(partial_value, ('dp', 'owner'))]
    all_to_all x1, blocking collectives: 79.7 us -> 52.7 us  [on_device(): lax.all_to_all(rounded, AXES, split_axis=0, concat_axis=0, tiled=True)]
    dot_general x4, matrix products: 42.8 us -> 26.1 us  [the longest x2 15.6 us: orthogonalize(): jnp.dot(current, poly_mat, preferred_element_type=jnp.float32)]
    scatter x1 -> x0, local copies, waits for them, and re-layouts: 16.3 us -> none  [on_device(): jnp.zeros((CAP * device_count, row_count, col_count), jnp.bfloat16)]
    reshape x2 -> x0, local copies, waits for them, and re-layouts: 10.1 us -> none  [the longest x1 6.37 us: on_device(): orthogonal.reshape(CAP, device_count, row_count, col_count)]
    all_to_all x2 -> x0, local copies, waits for them, and re-layouts: 6.43 us -> none  [route_rows(): lax.all_to_all(buffer, ('dp', 'owner'), split_axis=1, concat_axis=1, tile...]
  transfers between devices with their start and end apart: 1 -> 1, of which waited for: 1 -> 0; matrix products, arithmetic and copies ran while one was open for 0% -> 1% of each run, Pallas kernels for 0% -> 0%
where the time goes in v1:
time: 194 us
  blocking collectives  145 us (75%)
  matrix products  26.1 us (13%)
  other arithmetic  12 us (6%)
  starting transfers between devices  4.91 us (3%)
  local copies, waits for them, and re-layouts  3.64 us (2%)
  between operations  2.09 us (1%)
    unnamed x1, blocking collectives  92.1 us
    all_to_all x1, blocking collectives, on_device(): lax.all_to_all(rounded, AXES, split_axis=0, concat_axis=0, tiled=True)  52.7 us
    dot_general x2, matrix products, orthogonalize(): jnp.dot(current, poly_mat, preferred_element_type=jnp.float32)  15.6 us
    dot_general x2, matrix products, orthogonalize(): jnp.einsum('df,dg->fg', current, current, preferred_element_type=jnp.floa...  10.5 us
    convert_element_type x1, other arithmetic, on_device(): rounded = (grad_float + momentum_decay * fresh).astype(jnp.bfloat16)  7.79 us
    all_to_all x1, starting transfers between devices, on_device(): lax.all_to_all(scaled.reshape(matrices, row_count, col_count), AXES, spli...  4.91 us
  transfers between devices with their start and end apart: 1, of which 0 were waited for; matrix products, arithmetic and copies ran while one was open for 1% of the time, Pallas kernels for 0%

profile of v1, /device:TPU:1, one launch (start us, length us, event | category | flops | bytes accessed | tf_op | source)
XLA Modules:
  0.0 193.6 jit_solution(12960518624850931474)
XLA Ops:
  0.6 7.8 %fusion = (bf16[128,16,768]{2,1,0:T(8,128)(2,1)S(1)}, f32[128,16,768]{2,1,0:T(8,128)}) fusion(bf16[128,16,768]{2,1,0:T(8,128)(2,1)} %param.3, f32[128,16,768]{2,1,0:T(8,128)} %param.4), kind=kLoop, calls=%fused_computation.6 | loop fusion | flops 9437184 | bytes 18874368 | tf_op jit(solution)/shard_map/convert_element_type | solution.py:41
  8.4 52.7 %all_to_all.10 = bf16[128,16,768]{2,1,0:T(8,128)(2,1)S(1)} all-to-all(bf16[128,16,768]{2,1,0:T(8,128)(2,1)S(1)} %get-tuple-element.11), channel_id=1, replica_groups=mesh['dp'=4,'owner'=32] {'dp','owner'}, dimensions={0} | all-to-all | bytes 6291456 | tf_op jit(solution)/shard_map/all_to_all | solution.py:42
  61.1 2.2 %fusion.1 = f32[]{:T(128)} fusion(bf16[128,16,768]{2,1,0:T(8,128)(2,1)S(1)} %all_to_all.10), kind=kLoop, calls=%fused_computation.7 | loop fusion | flops 4718591 | bytes 3145732 | tf_op jit(solution)/shard_map/reduce_sum | solution.py:44
  64.0 1.0 fusion.2
  65.1 1.7 copy.22
  66.8 3.7 %bitcast_convert_fusion = bf16[768,768]{1,0:T(8,128)(2,1)} fusion(bf16[128,16,768]{2,0,1:T(8,128)(2,1)S(1)} %fusion.2), kind=kOutput, calls=%fused_computation.13 | convolution fusion | flops 2416508928 | bytes 4325376 | tf_op jit(solution)/shard_map/df,dg->fg/dot_general | solution.py:21
  70.5 7.4 %add_convert_fusion.1 = bf16[2048,768]{1,0:T(8,128)(2,1)} fusion(bf16[2048,768]{1,0:T(8,128)(2,1)S(1)} %bitcast.19, bf16[768,768]{1,0:T(8,128)(2,1)} %bitcast_convert_fusion), kind=kOutput, calls=%fused_computation.12 | convolution fusion | flops 3331129344 | bytes 7471104 | tf_op jit(solution)/shard_map/dot_general | solution.py:30
  77.9 0.0 copy-start.1
  77.9 6.9 %convolution_convert_fusion = bf16[768,768]{1,0:T(8,128)(2,1)} fusion(bf16[2048,768]{1,0:T(8,128)(2,1)} %add_convert_fusion.1), kind=kOutput, calls=%fused_computation.16 | convolution fusion | flops 2416508928 | bytes 4325376 | tf_op jit(solution)/shard_map/df,dg->fg/dot_general | solution.py:21
  84.7 0.0 copy-done.1
  84.7 8.2 %fusion.4 = (f32[]{:T(128)}, bf16[2048,768]{1,0:T(8,128)(2,1)}) fusion(bf16[2048,768]{1,0:T(8,128)(2,1)S(1)} %copy-done.1, bf16[768,768]{1,0:T(8,128)(2,1)} %convolution_convert_fusion), kind=kOutput, calls=%fused_computation.10 | convolution fusion | flops 3338993664 | bytes 7471108 | tf_op jit(solution)/shard_map/dot_general | solution.py:30
  93.0 0.0 copy-start
  93.0 4.9 %all-to-all-start.1 = ((bf16[128,16,768]{2,1,0:T(8,128)(2,1)}), bf16[128,16,768]{2,1,0:T(8,128)(2,1)S(1)}, u32[]{:S(2)}, u32[]{:S(2)}) async-start(bf16[128,16,768]{2,1,0:T(8,128)(2,1)} %bitcast.18), calls=%async_computation.1 | async-start | bytes 6291456 | tf_op jit(solution)/shard_map/all_to_all | solution.py:51
  97.9 0.0 copy-done
  97.9 0.1 copy.24
  98.0 0.2 reduce-window.8
  98.2 0.1 add_reduce_fusion
  99.0 0.1 dynamic-update-slice
  99.2 92.1 %all-reduce = f32[128]{0:T(128)S(1)} all-reduce(f32[128]{0:T(128)S(1)} %dynamic-update-slice), channel_id=1, replica_groups=mesh['dp'=4,'owner'=32] {'dp','owner'}, use_global_device_ids=true, to_apply=%add | all-reduce | flops 128 | bytes 1024
  191.3 0.6 fusion.5
  191.9 0.0 all-to-all-done.1
  191.9 1.7 copy.30
  (2 shorter events, 0.0 us)
Async XLA Ops:
  77.9 6.9 %copy-start.1 = (bf16[2048,768]{1,0:T(8,128)(2,1)S(1)}, bf16[2048,768]{1,0:T(8,128)(2,1)}, u32[]{:S(2)}) copy-start(bf16[2048,768]{1,0:T(8,128)(2,1)} %add_convert_fusion.1) | copy-start | bytes 9437188
  93.0 4.9 %copy-start = (s32[128]{0:T(128)S(1)}, s32[128]{0:T(128)}, u32[]{:S(2)}) copy-start(s32[128]{0:T(128)} %param.5) | copy-start | bytes 1540
  93.0 98.9 %all-to-all-start.1 = ((bf16[128,16,768]{2,1,0:T(8,128)(2,1)}), bf16[128,16,768]{2,1,0:T(8,128)(2,1)S(1)}, u32[]{:S(2)}, u32[]{:S(2)}) async-start(bf16[128,16,768]{2,1,0:T(8,128)(2,1)} %bitcast.18), calls=%async_computation.1 | async-start | bytes 6291456 | tf_op jit(solution)/shard_map/all_to_all | solution.py:51

commit v2 on v1

v2 whole, which is shorter than its diff:
```python
import math

import jax
import jax.numpy as jnp
from jax import lax
from jax.experimental import pallas as pl
from jax.experimental.pallas import tpu as pltpu
from jax.sharding import PartitionSpec as P

AXES = ("dp", "owner")
MESH = pl.DeviceIdType.MESH
F32, BF16 = jnp.float32, jnp.bfloat16
TRANSPOSED = (((0,), (0,)), ((), ()))

momentum_decay = 0.95
linear_coef = 3.4445
cubic_coef = -4.775
quintic_coef = 2.0315
norm_epsilon = 1e-07

DEVICES, CHIPS, CORES = 128, 64, 2
ROWS, FF = 16, 768
TILE = 256
CHUNKS = 4
GROUPS = 8
BLOCKS = 4


def displacement(step):
    n = lax.rem(step * 21, CHIPS)
    return lax.div(n, 16), lax.rem(lax.div(n, 4), 4), lax.rem(n, 4)


def kernel(
    g_hbm, m_hbm, table_ref, fresh_hbm, update_hbm, log_ref,
    gv, mv, rows, sent, gram, poly, total, rms_rows, rms_mine,
    load_sem, fresh_sem, send_sem, recv_sem, own_sem, back_send, back_recv, rms_send, rms_recv,
):
    y, o = lax.axis_index("dp"), lax.axis_index("owner")
    x, z, core = lax.div(o, 8), lax.rem(lax.div(o, 2), 4), lax.rem(o, 2)
    me = y * 32 + o
    sign = 1 - 2 * core

    def chip_at(step, direction):
        dy, dx, dz = displacement(step)
        ty = lax.rem(y + direction * dy + 4, 4)
        tx = lax.rem(x + direction * dx + 4, 4)
        tz = lax.rem(z + direction * dz + 4, 4)
        return ty, tx * 8 + tz * 2

    per = CHIPS // CHUNKS
    loads = []
    for phase in range(CORES):
        for k in range(CHUNKS):
            part = pl.ds(k * per, per)
            pair = (
                pltpu.make_async_copy(
                    g_hbm.at[part, phase], gv.at[part, phase], load_sem.at[0, phase, k]
                ),
                pltpu.make_async_copy(
                    m_hbm.at[part, phase], mv.at[part, phase], load_sem.at[1, phase, k]
                ),
            )
            for copy in pair:
                copy.start()
            loads.append(pair)

    barrier = pltpu.get_barrier_semaphore()

    def greet(i, carry):
        t = lax.rem(me + i, DEVICES)
        pl.semaphore_signal(
            barrier, inc=1, device_id=(lax.div(t, 32), lax.rem(t, 32)), device_id_type=MESH
        )
        return carry

    lax.fori_loop(1, DEVICES, greet, 0)

    def effective(phase):
        for k in range(CHUNKS):
            for copy in loads[phase * CHUNKS + k]:
                copy.wait()

            def one(i, carry):
                grad = gv[i, phase].astype(F32)
                fresh = momentum_decay * mv[i, phase] + grad
                mv[i, phase] = fresh
                gv[i, phase] = (grad + momentum_decay * fresh).astype(BF16)
                return carry

            lax.fori_loop(k * per, (k + 1) * per, one, 0)
            part = pl.ds(k * per, per)
            pltpu.make_async_copy(
                mv.at[part, phase], fresh_hbm.at[part, phase], fresh_sem.at[phase, k]
            ).start()

    def forward(phase):
        mine = y * 16 + x * 4 + z

        @pl.when(core != phase)
        def _():
            pltpu.make_async_remote_copy(
                src_ref=gv.at[mine, phase],
                dst_ref=rows.at[core],
                send_sem=send_sem,
                recv_sem=recv_sem.at[0],
                device_id=(y, x * 8 + z * 2 + phase),
                device_id_type=MESH,
            ).start()

        @pl.when(core == phase)
        def _():
            pltpu.make_async_copy(gv.at[mine, phase], rows.at[core], own_sem.at[0]).start()

        def one(step, carry):
            ty, to = chip_at(step, sign)
            pltpu.make_async_remote_copy(
                src_ref=gv.at[ty * 16 + lax.div(to, 2), phase],
                dst_ref=rows.at[2 * step + core],
                send_sem=send_sem,
                recv_sem=recv_sem.at[lax.div(step, CHIPS // GROUPS)],
                device_id=(ty, to + phase),
                device_id_type=MESH,
            ).start()
            return carry

        lax.fori_loop(1, CHIPS, one, 0)

    effective(0)
    pl.semaphore_wait(barrier, DEVICES - 1)
    forward(0)
    effective(1)
    forward(1)

    size = DEVICES // GROUPS
    total[...] = jnp.zeros_like(total)

    def accumulate(j):
        block = rows[pl.ds(j * size, size)].reshape(size * ROWS, FF)
        flipped = block.T
        for b in range(FF // TILE):
            n = TILE * (b + 1)
            total[0:n, TILE * b : n] += jnp.dot(
                flipped[0:n], block[:, TILE * b : n], preferred_element_type=F32
            )

    pltpu.make_async_copy(rows.at[0], rows.at[0], own_sem.at[0]).wait()
    pltpu.make_async_copy(
        rows.at[pl.ds(0, size - 1)], rows.at[pl.ds(0, size - 1)], recv_sem.at[0]
    ).wait()
    accumulate(0)

    def arrive(j, carry):
        part = rows.at[pl.ds(j * size, size)]
        pltpu.make_async_copy(part, part, recv_sem.at[j]).wait()
        accumulate(j)
        return carry

    lax.fori_loop(1, GROUPS, arrive, 0)

    on_diagonal = lax.broadcasted_iota(jnp.int32, (TILE, TILE), 0) == lax.broadcasted_iota(
        jnp.int32, (TILE, TILE), 1
    )
    squares = jnp.zeros((1, 1), F32)
    for b in range(FF // TILE):
        s = slice(TILE * b, TILE * (b + 1))
        squares += jnp.sum(jnp.where(on_diagonal, total[s, s], 0.0), keepdims=True)
    inverse = 1.0 / (jnp.sqrt(squares) + norm_epsilon)

    def mirror(b, upper):
        n = TILE * (b + 1)
        gram[0:n, TILE * b : n] = upper
        for a in range(b):
            gram[TILE * b : n, TILE * a : TILE * (a + 1)] = upper[TILE * a : TILE * (a + 1)].T

    for b in range(FF // TILE):
        n = TILE * (b + 1)
        mirror(b, (total[0:n, TILE * b : n] * inverse * inverse).astype(BF16))

    def polynomial():
        g = gram[...]
        square = jnp.dot(g, g, preferred_element_type=F32)
        poly[...] = (cubic_coef * g.astype(F32) + quintic_coef * square).astype(BF16)

    span = DEVICES // BLOCKS

    def apply(current):
        return (
            linear_coef * current.astype(F32)
            + jnp.dot(current, poly[...], preferred_element_type=F32)
        ).astype(BF16)

    polynomial()

    def first(j, carry):
        part = pl.ds(j * span, span)
        start = (rows[part].reshape(span * ROWS, FF).astype(F32) * inverse).astype(BF16)
        rows[part] = apply(start).reshape(span, ROWS, FF)
        return carry

    lax.fori_loop(0, BLOCKS, first, 0)

    whole = rows[...].reshape(DEVICES * ROWS, FF)
    for b in range(FF // TILE):
        n = TILE * (b + 1)
        mirror(
            b,
            lax.dot_general(
                whole[:, 0:n], whole[:, TILE * b : n], TRANSPOSED, preferred_element_type=F32
            ).astype(BF16),
        )
    polynomial()

    full_rows = DEVICES * ROWS

    def send_back(step, c):
        ty, to = chip_at(step, 2 * c - 1)
        pltpu.make_async_remote_copy(
            src_ref=sent.at[2 * step + c],
            dst_ref=update_hbm.at[me],
            send_sem=back_send,
            recv_sem=back_recv,
            device_id=(ty, to + c),
            device_id_type=MESH,
        ).start()

    def last(j, energy):
        part = pl.ds(j * span, span)
        ortho = apply(rows[part].reshape(span * ROWS, FF)).astype(F32)
        sent[part] = (math.sqrt(full_rows) * ortho).astype(BF16).reshape(span, ROWS, FF)
        energy += jnp.sum((ortho * ortho).reshape(-1, 8, FF), axis=0)

        @pl.when(j == 0)
        def _():
            for c in range(CORES):

                @pl.when(core == c)
                def _():
                    pltpu.make_async_copy(sent.at[c], update_hbm.at[me], own_sem.at[1]).start()

                @pl.when(core != c)
                def _():
                    send_back(0, c)

        def one(step, carry):
            for c in range(CORES):
                send_back(step, c)
            return carry

        steps = CHIPS // BLOCKS
        lax.fori_loop(jnp.maximum(j * steps, 1), (j + 1) * steps, one, 0)
        return energy

    energy = lax.fori_loop(0, BLOCKS, last, jnp.zeros((8, FF), F32))
    mean = jnp.sum(energy, keepdims=True) / (full_rows * FF)
    rms = math.sqrt(full_rows) * jnp.sqrt(mean)
    lane = lax.broadcasted_iota(jnp.int32, (1, DEVICES), 1)
    rms_mine[...] = jnp.where(lane == me, rms, 0.0)

    def tell(i, carry):
        t = lax.rem(me + i, DEVICES)
        pltpu.make_async_remote_copy(
            src_ref=rms_mine,
            dst_ref=rms_rows.at[me],
            send_sem=rms_send,
            recv_sem=rms_recv,
            device_id=(lax.div(t, 32), lax.rem(t, 32)),
            device_id_type=MESH,
        ).start()
        return carry

    lax.fori_loop(1, DEVICES, tell, 0)
    pltpu.make_async_copy(rms_mine, rms_rows.at[me], own_sem.at[2]).start()

    others = pl.ds(0, DEVICES - 1)
    pltpu.make_async_copy(rms_mine, rms_rows.at[me], own_sem.at[2]).wait()
    pltpu.make_async_copy(rms_rows.at[others], rms_rows.at[others], rms_recv).wait()
    pltpu.make_async_copy(rms_rows.at[others], rms_rows.at[others], rms_send).wait()

    every = jnp.sum(rms_rows[...], axis=0)
    owned = table_ref[...] == me
    low = jnp.min(jnp.where(owned, lane, DEVICES), keepdims=True)
    high = jnp.max(jnp.where(owned, lane, -1), keepdims=True)
    first_rms = jnp.sum(jnp.where(lane == low, every, 0.0), keepdims=True)
    second_rms = jnp.sum(jnp.where((lane == high) & (high > low), every, 0.0), keepdims=True)
    log_ref[...] = jnp.where(lane == 0, first_rms, jnp.where(lane == 1, second_rms, 0.0))

    for phase in range(CORES):
        for k in range(CHUNKS):
            part = pl.ds(k * per, per)
            pltpu.make_async_copy(
                mv.at[part, phase], fresh_hbm.at[part, phase], fresh_sem.at[phase, k]
            ).wait()
    pltpu.make_async_copy(rows.at[others], rows.at[others], send_sem).wait()
    pltpu.make_async_copy(sent.at[others], sent.at[others], back_send).wait()
    pltpu.make_async_copy(sent.at[0], update_hbm.at[me], own_sem.at[1]).wait()
    pltpu.make_async_copy(update_hbm.at[others], update_hbm.at[others], back_recv).wait()


def on_device(gradient, momentum, owner_table):
    paired = (CHIPS, CORES, ROWS, FF)
    anywhere = pl.BlockSpec(memory_space=pl.ANY)
    in_vmem = pl.BlockSpec(memory_space=pltpu.VMEM)
    fresh, update, log = pl.pallas_call(
        kernel,
        out_shape=(
            jax.ShapeDtypeStruct(paired, F32),
            jax.ShapeDtypeStruct((DEVICES, ROWS, FF), BF16),
            jax.ShapeDtypeStruct((1, DEVICES), F32),
        ),
        in_specs=[anywhere, anywhere, in_vmem],
        out_specs=(anywhere, anywhere, in_vmem),
        scratch_shapes=[
            pltpu.VMEM(paired, BF16),
            pltpu.VMEM(paired, F32),
            pltpu.VMEM((DEVICES, ROWS, FF), BF16),
            pltpu.VMEM((DEVICES, ROWS, FF), BF16),
            pltpu.VMEM((FF, FF), BF16),
            pltpu.VMEM((FF, FF), BF16),
            pltpu.VMEM((FF, FF), F32),
            pltpu.VMEM((DEVICES, 1, DEVICES), F32),
            pltpu.VMEM((1, DEVICES), F32),
            pltpu.SemaphoreType.DMA((2, CORES, CHUNKS)),
            pltpu.SemaphoreType.DMA((CORES, CHUNKS)),
            pltpu.SemaphoreType.DMA,
            pltpu.SemaphoreType.DMA((GROUPS,)),
            pltpu.SemaphoreType.DMA((3,)),
            pltpu.SemaphoreType.DMA,
            pltpu.SemaphoreType.DMA,
            pltpu.SemaphoreType.DMA,
            pltpu.SemaphoreType.DMA,
        ],
        compiler_params=pltpu.CompilerParams(
            collective_id=0, has_side_effects=True, vmem_limit_bytes=40 * 2**20
        ),
        cost_estimate=pl.CostEstimate(
            flops=11 * 10**9, bytes_accessed=18 * 2**20, transcendentals=0
        ),
        name="orthogonalize",
    )(
        gradient.reshape(paired),
        momentum.reshape(paired),
        owner_table.reshape(1, DEVICES),
    )
    return fresh.reshape(momentum.shape), update, log[:, :2]


def solution(mesh):
    split = P(None, AXES, None)
    return jax.shard_map(
        on_device,
        mesh=mesh,
        in_specs=(split, split, P()),
        out_specs=(split, split, P(AXES, None)),
        check_vma=False,
    )
```

time: 194 us -> 99.3 us (0.51)
  blocking collectives: 145 us -> 0 us
  Pallas kernels: 0 us -> 91.1 us
  matrix products: 26.1 us -> 0 us
  other arithmetic: 12 us -> 0 us
  starting transfers between devices: 4.91 us -> 0 us
  local copies, waits for them, and re-layouts: 3.64 us -> 7.42 us
    unnamed x1 -> x0, blocking collectives: 92.1 us -> none
    pallas_call x0 -> x1, Pallas kernels: none -> 91.1 us  [on_device(): pl.pallas_call(kernel, out_shape=(jax.ShapeDtypeStruct(paired, F32), jax....]
    all_to_all x1 -> x0, blocking collectives: 52.7 us -> none  [on_device(): lax.all_to_all(rounded, AXES, split_axis=0, concat_axis=0, tiled=True)]
    dot_general x4 -> x0, matrix products: 26.1 us -> none  [the longest x2 15.6 us: orthogonalize(): jnp.dot(current, poly_mat, preferred_element_type=jnp.float32)]
    convert_element_type x2 -> x0, other arithmetic: 8.84 us -> none  [the longest x1 7.79 us: on_device(): rounded = (grad_float + momentum_decay * fresh).astype(jnp.bfloat16)]
    unnamed x7, local copies, waits for them, and re-layouts: 1.79 us -> 7.42 us
    all_to_all x1 -> x0, starting transfers between devices: 4.91 us -> none  [on_device(): lax.all_to_all(scaled.reshape(matrices, row_count, col_count), AXES, spli...]
    reduce_sum x2 -> x0, other arithmetic: 2.85 us -> none  [the longest x1 2.22 us: on_device(): norm = jnp.sqrt(jnp.sum(whole * whole)) + norm_epsilon]
  transfers between devices with their start and end apart: 1 -> 0, of which waited for: 0 -> 0; matrix products, arithmetic and copies ran while one was open for 1% -> 0% of each run, Pallas kernels for 0% -> 0%
where the time goes in v2:
time: 99.3 us; the launch traced here: 99.2 us
  Pallas kernels  91.1 us (92%)
  local copies, waits for them, and re-layouts  7.42 us (7%)
    pallas_call x1, Pallas kernels, on_device(): pl.pallas_call(kernel, out_shape=(jax.ShapeDtypeStruct(paired, F32), jax....  91.1 us
    unnamed x7, local copies, waits for them, and re-layouts  7.42 us

profile of v2, /device:TPU:1, one launch (start us, length us, event | category | flops | bytes accessed | tf_op | source)
XLA Modules:
  0.0 99.2 jit_solution(2979193863640904774)
XLA Ops:
  0.6 0.0 copy-start
  0.6 1.9 %copy-done = bf16[128,16,768]{2,1,0:T(8,128)(2,1)S(1)} copy-done((bf16[128,16,768]{2,1,0:T(8,128)(2,1)S(1)}, bf16[128,16,768]{2,1,0:T(8,128)(2,1)}, u32[]{:S(2)}) %copy-start) | copy-done | bytes 3145752
  2.5 0.0 copy-start.1
  2.5 0.7 copy-done.1
  3.2 91.1 %orthogonalize.1 = (f32[64,2,16,768]{3,2,1,0:T(8,128)S(1)}, bf16[128,16,768]{2,1,0:T(8,128)(2,1)S(1)}, f32[1,128]{1,0:T(1,128)S(1)}) custom-call(bf16[64,2,16,768]{3,2,1,0:T(8,128)(2,1)S(1)} %bitcast.6, f32[64,2,16,768]{3,2,1,0:T(8,128)} %bitcast.9, s32[1,128]{1,0:T(1,128)S(1)} %bitcast.7), custom_call_target="tpu_custom_call" | custom-call | flops 11000000512 | bytes 18874368 | tf_op jit(solution)/shard_map/orthogonalize/pallas_call | solution.py:304
  94.3 2.7 %copy.9 = f32[128,16,768]{2,1,0:T(8,128)} copy(f32[128,16,768]{2,1,0:T(8,128)S(1)} %bitcast.5) | data formatting | bytes 12582912
  97.0 1.7 %copy.10 = bf16[128,16,768]{2,1,0:T(8,128)(2,1)} copy(bf16[128,16,768]{2,1,0:T(8,128)(2,1)S(1)} %get-tuple-element.13) | data formatting | bytes 6291456
  98.7 0.5 copy.11
Async XLA Ops:
  0.6 1.9 %copy-start = (bf16[128,16,768]{2,1,0:T(8,128)(2,1)S(1)}, bf16[128,16,768]{2,1,0:T(8,128)(2,1)}, u32[]{:S(2)}) copy-start(bf16[128,16,768]{2,1,0:T(8,128)(2,1)} %param.3) | copy-start | bytes 9437188
  2.5 0.7 copy-start.1

commit v3 on v2

--- a/solution.py
+++ b/solution.py
@@ -23,7 +23,10 @@
 TILE = 256
 CHUNKS = 4
 GROUPS = 8
-BLOCKS = 4
+STORES = 4
+CAP = 2
+HALVES = 2
+BLOCKS = CORES * HALVES
 
 
 def displacement(step):
@@ -32,8 +35,8 @@
 
 
 def kernel(
-    g_hbm, m_hbm, table_ref, fresh_hbm, update_hbm, log_ref,
-    gv, mv, rows, sent, gram, poly, total, rms_rows, rms_mine,
+    g_hbm, m_hbm, table_hbm, fresh_hbm, update_hbm, log_ref,
+    gv, mv, rows, sent, gram, poly, total, rms_rows, rms_mine, table,
     load_sem, fresh_sem, send_sem, recv_sem, own_sem, back_send, back_recv, rms_send, rms_recv,
 ):
     y, o = lax.axis_index("dp"), lax.axis_index("owner")
@@ -65,6 +68,9 @@
                 copy.start()
             loads.append(pair)
 
+    table_copy = pltpu.make_async_copy(table_hbm, table, own_sem.at[3])
+    table_copy.start()
+
     barrier = pltpu.get_barrier_semaphore()
 
     def greet(i, carry):
@@ -101,7 +107,7 @@
         def _():
             pltpu.make_async_remote_copy(
                 src_ref=gv.at[mine, phase],
-                dst_ref=rows.at[core],
+                dst_ref=rows.at[core, 0],
                 send_sem=send_sem,
                 recv_sem=recv_sem.at[0],
                 device_id=(y, x * 8 + z * 2 + phase),
@@ -110,13 +116,13 @@
 
         @pl.when(core == phase)
         def _():
-            pltpu.make_async_copy(gv.at[mine, phase], rows.at[core], own_sem.at[0]).start()
+            pltpu.make_async_copy(gv.at[mine, phase], rows.at[core, 0], own_sem.at[0]).start()
 
         def one(step, carry):
             ty, to = chip_at(step, sign)
             pltpu.make_async_remote_copy(
                 src_ref=gv.at[ty * 16 + lax.div(to, 2), phase],
-                dst_ref=rows.at[2 * step + core],
+                dst_ref=rows.at[core, step],
                 send_sem=send_sem,
                 recv_sem=recv_sem.at[lax.div(step, CHIPS // GROUPS)],
                 device_id=(ty, to + phase),
@@ -132,11 +138,11 @@
     effective(1)
     forward(1)
 
-    size = DEVICES // GROUPS
+    size = CHIPS // GROUPS
     total[...] = jnp.zeros_like(total)
 
     def accumulate(j):
-        block = rows[pl.ds(j * size, size)].reshape(size * ROWS, FF)
+        block = rows[:, pl.ds(j * size, size)].reshape(CORES * size * ROWS, FF)
         flipped = block.T
         for b in range(FF // TILE):
             n = TILE * (b + 1)
@@ -144,14 +150,13 @@
                 flipped[0:n], block[:, TILE * b : n], preferred_element_type=F32
             )
 
-    pltpu.make_async_copy(rows.at[0], rows.at[0], own_sem.at[0]).wait()
-    pltpu.make_async_copy(
-        rows.at[pl.ds(0, size - 1)], rows.at[pl.ds(0, size - 1)], recv_sem.at[0]
-    ).wait()
+    pltpu.make_async_copy(rows.at[0, 0], rows.at[0, 0], own_sem.at[0]).wait()
+    remote = rows.at[0, pl.ds(0, CORES * size - 1)]
+    pltpu.make_async_copy(remote, remote, recv_sem.at[0]).wait()
     accumulate(0)
 
     def arrive(j, carry):
-        part = rows.at[pl.ds(j * size, size)]
+        part = rows.at[:, pl.ds(j * size, size)]
         pltpu.make_async_copy(part, part, recv_sem.at[j]).wait()
         accumulate(j)
         return carry
@@ -182,7 +187,7 @@
         square = jnp.dot(g, g, preferred_element_type=F32)
         poly[...] = (cubic_coef * g.astype(F32) + quintic_coef * square).astype(BF16)
 
-    span = DEVICES // BLOCKS
+    span = CHIPS // HALVES
 
     def apply(current):
         return (
@@ -193,9 +198,9 @@
     polynomial()
 
     def first(j, carry):
-        part = pl.ds(j * span, span)
-        start = (rows[part].reshape(span * ROWS, FF).astype(F32) * inverse).astype(BF16)
-        rows[part] = apply(start).reshape(span, ROWS, FF)
+        core_of, part = lax.div(j, HALVES), pl.ds(lax.rem(j, HALVES) * span, span)
+        start = (rows[core_of, part].reshape(span * ROWS, FF).astype(F32) * inverse).astype(BF16)
+        rows[core_of, part] = apply(start).reshape(span, ROWS, FF)
         return carry
 
     lax.fori_loop(0, BLOCKS, first, 0)
@@ -216,7 +221,7 @@
     def send_back(step, c):
         ty, to = chip_at(step, 2 * c - 1)
         pltpu.make_async_remote_copy(
-            src_ref=sent.at[2 * step + c],
+            src_ref=sent.at[c, step],
             dst_ref=update_hbm.at[me],
             send_sem=back_send,
             recv_sem=back_recv,
@@ -225,30 +230,25 @@
         ).start()
 
     def last(j, energy):
-        part = pl.ds(j * span, span)
-        ortho = apply(rows[part].reshape(span * ROWS, FF)).astype(F32)
-        sent[part] = (math.sqrt(full_rows) * ortho).astype(BF16).reshape(span, ROWS, FF)
+        c, half = lax.div(j, HALVES), lax.rem(j, HALVES)
+        part = pl.ds(half * span, span)
+        ortho = apply(rows[c, part].reshape(span * ROWS, FF)).astype(F32)
+        sent[c, part] = (math.sqrt(full_rows) * ortho).astype(BF16).reshape(span, ROWS, FF)
         energy += jnp.sum((ortho * ortho).reshape(-1, 8, FF), axis=0)
 
-        @pl.when(j == 0)
+        @pl.when((half == 0) & (core == c))
         def _():
-            for c in range(CORES):
-
-                @pl.when(core == c)
-                def _():
-                    pltpu.make_async_copy(sent.at[c], update_hbm.at[me], own_sem.at[1]).start()
-
-                @pl.when(core != c)
-                def _():
-                    send_back(0, c)
+            pltpu.make_async_copy(sent.at[c, 0], update_hbm.at[me], own_sem.at[1]).start()
+
+        @pl.when((half == 0) & (core != c))
+        def _():
+            send_back(0, c)
 
         def one(step, carry):
-            for c in range(CORES):
-                send_back(step, c)
+            send_back(step, c)
             return carry
 
-        steps = CHIPS // BLOCKS
-        lax.fori_loop(jnp.maximum(j * steps, 1), (j + 1) * steps, one, 0)
+        lax.fori_loop(jnp.maximum(half * span, 1), (half + 1) * span, one, 0)
         return energy
 
     energy = lax.fori_loop(0, BLOCKS, last, jnp.zeros((8, FF), F32))
@@ -278,7 +278,8 @@
     pltpu.make_async_copy(rms_rows.at[others], rms_rows.at[others], rms_send).wait()
 
     every = jnp.sum(rms_rows[...], axis=0)
-    owned = table_ref[...] == me
+    table_copy.wait()
+    owned = table[...] == me
     low = jnp.min(jnp.where(owned, lane, DEVICES), keepdims=True)
     high = jnp.max(jnp.where(owned, lane, -1), keepdims=True)
     first_rms = jnp.sum(jnp.where(lane == low, every, 0.0), keepdims=True)
@@ -291,16 +292,31 @@
             pltpu.make_async_copy(
                 mv.at[part, phase], fresh_hbm.at[part, phase], fresh_sem.at[phase, k]
             ).wait()
-    pltpu.make_async_copy(rows.at[others], rows.at[others], send_sem).wait()
-    pltpu.make_async_copy(sent.at[others], sent.at[others], back_send).wait()
-    pltpu.make_async_copy(sent.at[0], update_hbm.at[me], own_sem.at[1]).wait()
+    pltpu.make_async_copy(update_hbm.at[others], update_hbm.at[others], send_sem).wait()
+    pltpu.make_async_copy(update_hbm.at[others], update_hbm.at[others], back_send).wait()
+    pltpu.make_async_copy(sent.at[0, 0], update_hbm.at[me], own_sem.at[1]).wait()
     pltpu.make_async_copy(update_hbm.at[others], update_hbm.at[others], back_recv).wait()
+
+
+def store(fresh_ref, update_ref, log_ref, fresh_out, update_out, log_out, sem):
+    per = DEVICES // STORES
+    copies = []
+    for k in range(STORES):
+        part = pl.ds(k * per, per)
+        copies.append(pltpu.make_async_copy(fresh_ref.at[part], fresh_out.at[part], sem.at[0, k]))
+        copies.append(pltpu.make_async_copy(update_ref.at[part], update_out.at[part], sem.at[1, k]))
+    for copy in copies:
+        copy.start()
+    log_out[...] = log_ref[:, :CAP]
+    for copy in copies:
+        copy.wait()
 
 
 def on_device(gradient, momentum, owner_table):
     paired = (CHIPS, CORES, ROWS, FF)
     anywhere = pl.BlockSpec(memory_space=pl.ANY)
     in_vmem = pl.BlockSpec(memory_space=pltpu.VMEM)
+    in_hbm = pl.BlockSpec(memory_space=pltpu.HBM)
     fresh, update, log = pl.pallas_call(
         kernel,
         out_shape=(
@@ -308,23 +324,24 @@
             jax.ShapeDtypeStruct((DEVICES, ROWS, FF), BF16),
             jax.ShapeDtypeStruct((1, DEVICES), F32),
         ),
-        in_specs=[anywhere, anywhere, in_vmem],
+        in_specs=[in_hbm, in_hbm, in_hbm],
         out_specs=(anywhere, anywhere, in_vmem),
         scratch_shapes=[
             pltpu.VMEM(paired, BF16),
             pltpu.VMEM(paired, F32),
-            pltpu.VMEM((DEVICES, ROWS, FF), BF16),
-            pltpu.VMEM((DEVICES, ROWS, FF), BF16),
+            pltpu.VMEM((CORES, CHIPS, ROWS, FF), BF16),
+            pltpu.VMEM((CORES, CHIPS, ROWS, FF), BF16),
             pltpu.VMEM((FF, FF), BF16),
             pltpu.VMEM((FF, FF), BF16),
             pltpu.VMEM((FF, FF), F32),
             pltpu.VMEM((DEVICES, 1, DEVICES), F32),
             pltpu.VMEM((1, DEVICES), F32),
+            pltpu.VMEM((1, DEVICES), jnp.int32),
             pltpu.SemaphoreType.DMA((2, CORES, CHUNKS)),
             pltpu.SemaphoreType.DMA((CORES, CHUNKS)),
             pltpu.SemaphoreType.DMA,
             pltpu.SemaphoreType.DMA((GROUPS,)),
-            pltpu.SemaphoreType.DMA((3,)),
+            pltpu.SemaphoreType.DMA((4,)),
             pltpu.SemaphoreType.DMA,
             pltpu.SemaphoreType.DMA,
             pltpu.SemaphoreType.DMA,
@@ -338,11 +355,23 @@
         ),
         name="orthogonalize",
     )(
-        gradient.reshape(paired),
-        momentum.reshape(paired),
-        owner_table.reshape(1, DEVICES),
+        pltpu.with_memory_space_constraint(gradient.reshape(paired), pltpu.HBM),
+        pltpu.with_memory_space_constraint(momentum.reshape(paired), pltpu.HBM),
+        pltpu.with_memory_space_constraint(owner_table.reshape(1, DEVICES), pltpu.HBM),
     )
-    return fresh.reshape(momentum.shape), update, log[:, :2]
+    return pl.pallas_call(
+        store,
+        out_shape=(
+            jax.ShapeDtypeStruct(momentum.shape, F32),
+            jax.ShapeDtypeStruct(update.shape, BF16),
+            jax.ShapeDtypeStruct((1, CAP), F32),
+        ),
+        in_specs=[anywhere, anywhere, in_vmem],
+        out_specs=(in_hbm, in_hbm, in_vmem),
+        scratch_shapes=[pltpu.SemaphoreType.DMA((2, STORES))],
+        compiler_params=pltpu.CompilerParams(vmem_limit_bytes=2**20),
+        name="store",
+    )(fresh.reshape(momentum.shape), update, log)
 
 
 def solution(mesh):

time: 99.3 us -> 95.7 us (0.964)
  local copies, waits for them, and re-layouts: 7.42 us -> 0 us
  Pallas kernels: 91.1 us -> 94 us
    unnamed x7 -> x0, local copies, waits for them, and re-layouts: 7.42 us -> none
    pallas_call x0 -> x1, Pallas kernels: none -> 4.2 us  [on_device(): pl.pallas_call(store, out_shape=(jax.ShapeDtypeStruct(momentum.shape, F32...]
    pallas_call x1, Pallas kernels: 91.1 us -> 89.8 us  [on_device(): pl.pallas_call(kernel, out_shape=(jax.ShapeDtypeStruct(paired, F32), jax....]
where the time goes in v3:
time: 95.7 us; the launch traced here: 94.7 us
  Pallas kernels  94 us (98%)
    pallas_call x1, Pallas kernels, on_device(): pl.pallas_call(kernel, out_shape=(jax.ShapeDtypeStruct(paired, F32), jax....  89.8 us
    pallas_call x1, Pallas kernels, on_device(): pl.pallas_call(store, out_shape=(jax.ShapeDtypeStruct(momentum.shape, F32...  4.2 us

profile of v3, /device:TPU:1, one launch (start us, length us, event | category | flops | bytes accessed | tf_op | source)
XLA Modules:
  0.0 94.7 jit_solution(6562405151188093171)
XLA Ops:
  0.6 89.8 %orthogonalize.1 = (f32[64,2,16,768]{3,2,1,0:T(8,128)S(1)}, bf16[128,16,768]{2,1,0:T(8,128)(2,1)S(1)}, f32[1,128]{1,0:T(1,128)S(1)}) custom-call(bf16[64,2,16,768]{3,2,1,0:T(8,128)(2,1)} %bitcast.6, f32[64,2,16,768]{3,2,1,0:T(8,128)} %bitcast.5, s32[1,128]{1,0:T(1,128)} %bitcast.7), custom_call_target="tpu_custom_call" | custom-call | flops 11000000512 | bytes 18874368 | tf_op jit(solution)/shard_map/orthogonalize/pallas_call | solution.py:320
  90.5 4.2 %store.1 = (f32[128,16,768]{2,1,0:T(8,128)}, bf16[128,16,768]{2,1,0:T(8,128)(2,1)}, f32[1,2]{1,0:T(1,128)}) custom-call(f32[128,16,768]{2,1,0:T(8,128)S(1)} %bitcast.4, bf16[128,16,768]{2,1,0:T(8,128)(2,1)S(1)} %get-tuple-element.7.update_ref, f32[1,128]{1,0:T(1,128)S(1)} %get-tuple-element.8.log_ref), custom_call_target="tpu_custom_call" | custom-call | tf_op jit(solution)/shard_map/store/pallas_call | solution.py:362

commit v4 on v3

--- a/solution.py
+++ b/solution.py
@@ -36,7 +36,7 @@
 
 def kernel(
     g_hbm, m_hbm, table_hbm, fresh_hbm, update_hbm, log_ref,
-    gv, mv, rows, sent, gram, poly, total, rms_rows, rms_mine, table,
+    gv, mv, rows, sent, gram, poly, total, rms_rows, table,
     load_sem, fresh_sem, send_sem, recv_sem, own_sem, back_send, back_recv, rms_send, rms_recv,
 ):
     y, o = lax.axis_index("dp"), lax.axis_index("owner")
@@ -68,7 +68,7 @@
                 copy.start()
             loads.append(pair)
 
-    table_copy = pltpu.make_async_copy(table_hbm, table, own_sem.at[3])
+    table_copy = pltpu.make_async_copy(table_hbm, table, own_sem.at[2])
     table_copy.start()
 
     barrier = pltpu.get_barrier_semaphore()
@@ -218,6 +218,8 @@
 
     full_rows = DEVICES * ROWS
 
+    lane = lax.broadcasted_iota(jnp.int32, (1, DEVICES), 1)
+
     def send_back(step, c):
         ty, to = chip_at(step, 2 * c - 1)
         pltpu.make_async_remote_copy(
@@ -229,53 +231,83 @@
             device_id_type=MESH,
         ).start()
 
+    def send_half(c, half):
+        if half == 0:
+
+            @pl.when(core == c)
+            def _():
+                pltpu.make_async_copy(sent.at[c, 0], update_hbm.at[me], own_sem.at[1]).start()
+
+            @pl.when(core != c)
+            def _():
+                send_back(0, c)
+
+        def one(step, carry):
+            send_back(step, c)
+            return carry
+
+        lax.fori_loop(max(half * span, 1), (half + 1) * span, one, 0)
+
     def last(j, energy):
         c, half = lax.div(j, HALVES), lax.rem(j, HALVES)
         part = pl.ds(half * span, span)
         ortho = apply(rows[c, part].reshape(span * ROWS, FF)).astype(F32)
         sent[c, part] = (math.sqrt(full_rows) * ortho).astype(BF16).reshape(span, ROWS, FF)
         energy += jnp.sum((ortho * ortho).reshape(-1, 8, FF), axis=0)
-
-        @pl.when((half == 0) & (core == c))
-        def _():
-            pltpu.make_async_copy(sent.at[c, 0], update_hbm.at[me], own_sem.at[1]).start()
-
-        @pl.when((half == 0) & (core != c))
-        def _():
-            send_back(0, c)
-
-        def one(step, carry):
-            send_back(step, c)
-            return carry
-
-        lax.fori_loop(jnp.maximum(half * span, 1), (half + 1) * span, one, 0)
+        pl.when(j == 0)(lambda: send_half(0, 0))
         return energy
 
     energy = lax.fori_loop(0, BLOCKS, last, jnp.zeros((8, FF), F32))
     mean = jnp.sum(energy, keepdims=True) / (full_rows * FF)
     rms = math.sqrt(full_rows) * jnp.sqrt(mean)
-    lane = lax.broadcasted_iota(jnp.int32, (1, DEVICES), 1)
-    rms_mine[...] = jnp.where(lane == me, rms, 0.0)
-
-    def tell(i, carry):
-        t = lax.rem(me + i, DEVICES)
+    rms_rows[me] = jnp.where(lane == me, rms, 0.0)
+
+    column, place = lax.div(me, 8), lax.rem(me, 8)
+    mine_too = pl.ds(column * 8, 8)
+    for i in range(1, 8):
         pltpu.make_async_remote_copy(
-            src_ref=rms_mine,
+            src_ref=rms_rows.at[me],
             dst_ref=rms_rows.at[me],
-            send_sem=rms_send,
-            recv_sem=rms_recv,
-            device_id=(lax.div(t, 32), lax.rem(t, 32)),
+            send_sem=rms_send.at[0],
+            recv_sem=rms_recv.at[0],
+            device_id=(y, x * 8 + lax.rem(place + i, 8)),
             device_id_type=MESH,
         ).start()
-        return carry
-
-    lax.fori_loop(1, DEVICES, tell, 0)
-    pltpu.make_async_copy(rms_mine, rms_rows.at[me], own_sem.at[2]).start()
+
+    def spread():
+        seven = rms_rows.at[pl.ds(0, 7)]
+        pltpu.make_async_copy(seven, seven, rms_recv.at[0]).wait()
+        for i in range(1, 16):
+            other = lax.rem(column + i, 16)
+            pltpu.make_async_remote_copy(
+                src_ref=rms_rows.at[mine_too],
+                dst_ref=rms_rows.at[mine_too],
+                send_sem=rms_send.at[1],
+                recv_sem=rms_recv.at[1],
+                device_id=(lax.div(other, 4), lax.rem(other, 4) * 8 + place),
+                device_id_type=MESH,
+            ).start()
+
+    send_half(0, 1)
+
+    @pl.when(core == 0)
+    def _():
+        send_half(1, 0)
+        send_half(1, 1)
+        spread()
+
+    @pl.when(core == 1)
+    def _():
+        spread()
+        send_half(1, 0)
+        send_half(1, 1)
 
     others = pl.ds(0, DEVICES - 1)
-    pltpu.make_async_copy(rms_mine, rms_rows.at[me], own_sem.at[2]).wait()
-    pltpu.make_async_copy(rms_rows.at[others], rms_rows.at[others], rms_recv).wait()
-    pltpu.make_async_copy(rms_rows.at[others], rms_rows.at[others], rms_send).wait()
+    for stage, count in ((0, 7), (1, DEVICES - 8)):
+        part = rms_rows.at[pl.ds(0, count)]
+        pltpu.make_async_copy(part, part, rms_send.at[stage]).wait()
+        if stage:
+            pltpu.make_async_copy(part, part, rms_recv.at[stage]).wait()
 
     every = jnp.sum(rms_rows[...], axis=0)
     table_copy.wait()
@@ -335,17 +367,16 @@
             pltpu.VMEM((FF, FF), BF16),
             pltpu.VMEM((FF, FF), F32),
             pltpu.VMEM((DEVICES, 1, DEVICES), F32),
-            pltpu.VMEM((1, DEVICES), F32),
             pltpu.VMEM((1, DEVICES), jnp.int32),
             pltpu.SemaphoreType.DMA((2, CORES, CHUNKS)),
             pltpu.SemaphoreType.DMA((CORES, CHUNKS)),
             pltpu.SemaphoreType.DMA,
             pltpu.SemaphoreType.DMA((GROUPS,)),
-            pltpu.SemaphoreType.DMA((4,)),
+            pltpu.SemaphoreType.DMA((3,)),
             pltpu.SemaphoreType.DMA,
             pltpu.SemaphoreType.DMA,
-            pltpu.SemaphoreType.DMA,
-            pltpu.SemaphoreType.DMA,
+            pltpu.SemaphoreType.DMA((2,)),
+            pltpu.SemaphoreType.DMA((2,)),
         ],
         compiler_params=pltpu.CompilerParams(
             collective_id=0, has_side_effects=True, vmem_limit_bytes=40 * 2**20

time: 95.7 us -> 94 us (0.982)
  no operation moved by 1% of the time
where the time goes in v4:
time: 94 us; the launch traced here: 93.9 us
  Pallas kernels  93.2 us (99%)
    pallas_call x1, Pallas kernels, on_device(): pl.pallas_call(kernel, out_shape=(jax.ShapeDtypeStruct(paired, F32), jax....  89 us
    pallas_call x1, Pallas kernels, on_device(): pl.pallas_call(store, out_shape=(jax.ShapeDtypeStruct(momentum.shape, F32...  4.2 us

profile of v4, /device:TPU:1, one launch (start us, length us, event | category | flops | bytes accessed | tf_op | source)
XLA Modules:
  0.0 93.9 jit_solution(2309127076110925529)
XLA Ops:
  0.6 89.0 %orthogonalize.1 = (f32[64,2,16,768]{3,2,1,0:T(8,128)S(1)}, bf16[128,16,768]{2,1,0:T(8,128)(2,1)S(1)}, f32[1,128]{1,0:T(1,128)S(1)}) custom-call(bf16[64,2,16,768]{3,2,1,0:T(8,128)(2,1)} %bitcast.6, f32[64,2,16,768]{3,2,1,0:T(8,128)} %bitcast.5, s32[1,128]{1,0:T(1,128)} %bitcast.7), custom_call_target="tpu_custom_call" | custom-call | flops 11000000512 | bytes 18874368 | tf_op jit(solution)/shard_map/orthogonalize/pallas_call | solution.py:352
  89.7 4.2 %store.1 = (f32[128,16,768]{2,1,0:T(8,128)}, bf16[128,16,768]{2,1,0:T(8,128)(2,1)}, f32[1,2]{1,0:T(1,128)}) custom-call(f32[128,16,768]{2,1,0:T(8,128)S(1)} %bitcast.4, bf16[128,16,768]{2,1,0:T(8,128)(2,1)S(1)} %get-tuple-element.7.update_ref, f32[1,128]{1,0:T(1,128)S(1)} %get-tuple-element.8.log_ref), custom_call_target="tpu_custom_call" | custom-call | tf_op jit(solution)/shard_map/store/pallas_call | solution.py:393

commit v5 on v4

--- a/solution.py
+++ b/solution.py
@@ -35,8 +35,8 @@
 
 
 def kernel(
-    g_hbm, m_hbm, table_hbm, fresh_hbm, update_hbm, log_ref,
-    gv, mv, rows, sent, gram, poly, total, rms_rows, table,
+    g_hbm, m_hbm, table_hbm, fresh_hbm, update_hbm, log_hbm,
+    gv, mv, rows, sent, gram, poly, total, rms_rows, table, log,
     load_sem, fresh_sem, send_sem, recv_sem, own_sem, back_send, back_recv, rms_send, rms_recv,
 ):
     y, o = lax.axis_index("dp"), lax.axis_index("owner")
@@ -50,6 +50,17 @@
         tx = lax.rem(x + direction * dx + 4, 4)
         tz = lax.rem(z + direction * dz + 4, 4)
         return ty, tx * 8 + tz * 2
+
+    barrier = pltpu.get_barrier_semaphore()
+
+    def greet(i, carry):
+        t = lax.rem(me + i, DEVICES)
+        pl.semaphore_signal(
+            barrier, inc=1, device_id=(lax.div(t, 32), lax.rem(t, 32)), device_id_type=MESH
+        )
+        return carry
+
+    lax.fori_loop(1, DEVICES, greet, 0)
 
     per = CHIPS // CHUNKS
     loads = []
@@ -71,17 +82,6 @@
     table_copy = pltpu.make_async_copy(table_hbm, table, own_sem.at[2])
     table_copy.start()
 
-    barrier = pltpu.get_barrier_semaphore()
-
-    def greet(i, carry):
-        t = lax.rem(me + i, DEVICES)
-        pl.semaphore_signal(
-            barrier, inc=1, device_id=(lax.div(t, 32), lax.rem(t, 32)), device_id_type=MESH
-        )
-        return carry
-
-    lax.fori_loop(1, DEVICES, greet, 0)
-
     def effective(phase):
         for k in range(CHUNKS):
             for copy in loads[phase * CHUNKS + k]:
@@ -172,20 +172,24 @@
         squares += jnp.sum(jnp.where(on_diagonal, total[s, s], 0.0), keepdims=True)
     inverse = 1.0 / (jnp.sqrt(squares) + norm_epsilon)
 
-    def mirror(b, upper):
+    def mirror(ref, b, upper):
         n = TILE * (b + 1)
-        gram[0:n, TILE * b : n] = upper
+        ref[0:n, TILE * b : n] = upper
         for a in range(b):
-            gram[TILE * b : n, TILE * a : TILE * (a + 1)] = upper[TILE * a : TILE * (a + 1)].T
+            ref[TILE * b : n, TILE * a : TILE * (a + 1)] = upper[TILE * a : TILE * (a + 1)].T
 
     for b in range(FF // TILE):
         n = TILE * (b + 1)
-        mirror(b, (total[0:n, TILE * b : n] * inverse * inverse).astype(BF16))
+        mirror(gram, b, (total[0:n, TILE * b : n] * inverse * inverse).astype(BF16))
 
     def polynomial():
-        g = gram[...]
-        square = jnp.dot(g, g, preferred_element_type=F32)
-        poly[...] = (cubic_coef * g.astype(F32) + quintic_coef * square).astype(BF16)
+        for b in range(FF // TILE):
+            n = TILE * (b + 1)
+            square = jnp.dot(gram[0:n, :], gram[:, TILE * b : n], preferred_element_type=F32)
+            upper = (
+                cubic_coef * gram[0:n, TILE * b : n].astype(F32) + quintic_coef * square
+            ).astype(BF16)
+            mirror(poly, b, upper)
 
     span = CHIPS // HALVES
 
@@ -197,18 +201,18 @@
 
     polynomial()
 
-    def first(j, carry):
-        core_of, part = lax.div(j, HALVES), pl.ds(lax.rem(j, HALVES) * span, span)
-        start = (rows[core_of, part].reshape(span * ROWS, FF).astype(F32) * inverse).astype(BF16)
-        rows[core_of, part] = apply(start).reshape(span, ROWS, FF)
+    def first(c, carry):
+        start = (rows[c].reshape(CHIPS * ROWS, FF).astype(F32) * inverse).astype(BF16)
+        rows[c] = apply(start).reshape(CHIPS, ROWS, FF)
         return carry
 
-    lax.fori_loop(0, BLOCKS, first, 0)
+    lax.fori_loop(0, CORES, first, 0)
 
     whole = rows[...].reshape(DEVICES * ROWS, FF)
     for b in range(FF // TILE):
         n = TILE * (b + 1)
         mirror(
+            gram,
             b,
             lax.dot_general(
                 whole[:, 0:n], whole[:, TILE * b : n], TRANSPOSED, preferred_element_type=F32
@@ -316,7 +320,9 @@
     high = jnp.max(jnp.where(owned, lane, -1), keepdims=True)
     first_rms = jnp.sum(jnp.where(lane == low, every, 0.0), keepdims=True)
     second_rms = jnp.sum(jnp.where((lane == high) & (high > low), every, 0.0), keepdims=True)
-    log_ref[...] = jnp.where(lane == 0, first_rms, jnp.where(lane == 1, second_rms, 0.0))
+    log[...] = jnp.where(lane == 0, first_rms, jnp.where(lane == 1, second_rms, 0.0))[:, :CAP]
+    log_copy = pltpu.make_async_copy(log, log_hbm, own_sem.at[3])
+    log_copy.start()
 
     for phase in range(CORES):
         for k in range(CHUNKS):
@@ -328,18 +334,18 @@
     pltpu.make_async_copy(update_hbm.at[others], update_hbm.at[others], back_send).wait()
     pltpu.make_async_copy(sent.at[0, 0], update_hbm.at[me], own_sem.at[1]).wait()
     pltpu.make_async_copy(update_hbm.at[others], update_hbm.at[others], back_recv).wait()
+    log_copy.wait()
 
 
 def store(fresh_ref, update_ref, log_ref, fresh_out, update_out, log_out, sem):
     per = DEVICES // STORES
-    copies = []
+    copies = [pltpu.make_async_copy(log_ref, log_out, sem.at[2, 0])]
     for k in range(STORES):
         part = pl.ds(k * per, per)
         copies.append(pltpu.make_async_copy(fresh_ref.at[part], fresh_out.at[part], sem.at[0, k]))
         copies.append(pltpu.make_async_copy(update_ref.at[part], update_out.at[part], sem.at[1, k]))
     for copy in copies:
         copy.start()
-    log_out[...] = log_ref[:, :CAP]
     for copy in copies:
         copy.wait()
 
@@ -347,17 +353,16 @@
 def on_device(gradient, momentum, owner_table):
     paired = (CHIPS, CORES, ROWS, FF)
     anywhere = pl.BlockSpec(memory_space=pl.ANY)
-    in_vmem = pl.BlockSpec(memory_space=pltpu.VMEM)
     in_hbm = pl.BlockSpec(memory_space=pltpu.HBM)
     fresh, update, log = pl.pallas_call(
         kernel,
         out_shape=(
             jax.ShapeDtypeStruct(paired, F32),
             jax.ShapeDtypeStruct((DEVICES, ROWS, FF), BF16),
-            jax.ShapeDtypeStruct((1, DEVICES), F32),
+            jax.ShapeDtypeStruct((1, CAP), F32),
         ),
         in_specs=[in_hbm, in_hbm, in_hbm],
-        out_specs=(anywhere, anywhere, in_vmem),
+        out_specs=(anywhere, anywhere, anywhere),
         scratch_shapes=[
             pltpu.VMEM(paired, BF16),
             pltpu.VMEM(paired, F32),
@@ -368,11 +373,12 @@
             pltpu.VMEM((FF, FF), F32),
             pltpu.VMEM((DEVICES, 1, DEVICES), F32),
             pltpu.VMEM((1, DEVICES), jnp.int32),
+            pltpu.VMEM((1, CAP), F32),
             pltpu.SemaphoreType.DMA((2, CORES, CHUNKS)),
             pltpu.SemaphoreType.DMA((CORES, CHUNKS)),
             pltpu.SemaphoreType.DMA,
             pltpu.SemaphoreType.DMA((GROUPS,)),
-            pltpu.SemaphoreType.DMA((3,)),
+            pltpu.SemaphoreType.DMA((4,)),
             pltpu.SemaphoreType.DMA,
             pltpu.SemaphoreType.DMA,
             pltpu.SemaphoreType.DMA((2,)),
@@ -397,9 +403,9 @@
             jax.ShapeDtypeStruct(update.shape, BF16),
             jax.ShapeDtypeStruct((1, CAP), F32),
         ),
-        in_specs=[anywhere, anywhere, in_vmem],
-        out_specs=(in_hbm, in_hbm, in_vmem),
-        scratch_shapes=[pltpu.SemaphoreType.DMA((2, STORES))],
+        in_specs=[anywhere, anywhere, anywhere],
+        out_specs=(in_hbm, in_hbm, in_hbm),
+        scratch_shapes=[pltpu.SemaphoreType.DMA((3, STORES))],
         compiler_params=pltpu.CompilerParams(vmem_limit_bytes=2**20),
         name="store",
     )(fresh.reshape(momentum.shape), update, log)

time: 94 us -> 93.2 us (level)
  no operation moved by 1% of the time
where the time goes in v5:
time: 93.2 us; the launch traced here: 93 us
  Pallas kernels  92.3 us (99%)
    pallas_call x1, Pallas kernels, on_device(): pl.pallas_call(kernel, out_shape=(jax.ShapeDtypeStruct(paired, F32), jax....  88.6 us
    pallas_call x1, Pallas kernels, on_device(): pl.pallas_call(store, out_shape=(jax.ShapeDtypeStruct(momentum.shape, F32...  3.73 us

profile of v5, /device:TPU:1, one launch (start us, length us, event | category | flops | bytes accessed | tf_op | source)
XLA Modules:
  0.0 93.0 jit_solution(2707527951343107240)
XLA Ops:
  0.6 88.6 %orthogonalize.1 = (f32[64,2,16,768]{3,2,1,0:T(8,128)S(1)}, bf16[128,16,768]{2,1,0:T(8,128)(2,1)S(1)}, f32[1,2]{1,0:T(1,128)S(1)}) custom-call(bf16[64,2,16,768]{3,2,1,0:T(8,128)(2,1)} %bitcast.6, f32[64,2,16,768]{3,2,1,0:T(8,128)} %bitcast.5, s32[1,128]{1,0:T(1,128)} %bitcast.7), custom_call_target="tpu_custom_call" | custom-call | flops 11000000512 | bytes 18874368 | tf_op jit(solution)/shard_map/orthogonalize/pallas_call | solution.py:357
  89.2 3.7 %store.1 = (f32[128,16,768]{2,1,0:T(8,128)}, bf16[128,16,768]{2,1,0:T(8,128)(2,1)}, f32[1,2]{1,0:T(1,128)}) custom-call(f32[128,16,768]{2,1,0:T(8,128)S(1)} %bitcast.4, bf16[128,16,768]{2,1,0:T(8,128)(2,1)S(1)} %get-tuple-element.7.update_ref, f32[1,2]{1,0:T(1,128)S(1)} %get-tuple-element.8.log_ref), custom_call_target="tpu_custom_call" | custom-call | tf_op jit(solution)/shard_map/store/pallas_call | solution.py:399

commit v6 on v5

--- a/solution.py
+++ b/solution.py
@@ -53,32 +53,41 @@
 
     barrier = pltpu.get_barrier_semaphore()
 
-    def greet(i, carry):
-        t = lax.rem(me + i, DEVICES)
-        pl.semaphore_signal(
-            barrier, inc=1, device_id=(lax.div(t, 32), lax.rem(t, 32)), device_id_type=MESH
-        )
-        return carry
-
-    lax.fori_loop(1, DEVICES, greet, 0)
-
     per = CHIPS // CHUNKS
     loads = []
     for phase in range(CORES):
         for k in range(CHUNKS):
             part = pl.ds(k * per, per)
-            pair = (
-                pltpu.make_async_copy(
-                    g_hbm.at[part, phase], gv.at[part, phase], load_sem.at[0, phase, k]
-                ),
-                pltpu.make_async_copy(
-                    m_hbm.at[part, phase], mv.at[part, phase], load_sem.at[1, phase, k]
-                ),
+            loads.append(
+                (
+                    pltpu.make_async_copy(
+                        g_hbm.at[part, phase], gv.at[part, phase], load_sem.at[0, phase, k]
+                    ),
+                    pltpu.make_async_copy(
+                        m_hbm.at[part, phase], mv.at[part, phase], load_sem.at[1, phase, k]
+                    ),
+                )
             )
+
+    def load(phase):
+        for pair in loads[phase * CHUNKS : (phase + 1) * CHUNKS]:
             for copy in pair:
                 copy.start()
-            loads.append(pair)
-
+
+    load(0)
+
+    for dy in range(4):
+        ty = lax.rem(y + dy, 4)
+
+        def greet(i, carry):
+            pl.semaphore_signal(
+                barrier, inc=1, device_id=(ty, lax.rem(o + i, 32)), device_id_type=MESH
+            )
+            return carry
+
+        lax.fori_loop(0 if dy else 1, 32, greet, 0)
+
+    load(1)
     table_copy = pltpu.make_async_copy(table_hbm, table, own_sem.at[2])
     table_copy.start()
 

time: 93.2 us -> 95.9 us (1.029)
  the two profiles are of different devices: /device:TPU:1 before, /device:TPU:25 now
where the time goes in v6:
time: 95.9 us; the launch traced here: 95.8 us
  Pallas kernels  95.2 us (99%)
    pallas_call x1, Pallas kernels, on_device(): pl.pallas_call(kernel, out_shape=(jax.ShapeDtypeStruct(paired, F32), jax....  91.5 us
    pallas_call x1, Pallas kernels, on_device(): pl.pallas_call(store, out_shape=(jax.ShapeDtypeStruct(momentum.shape, F32...  3.73 us

profile of v6, /device:TPU:25, one launch (start us, length us, event | category | flops | bytes accessed | tf_op | source)
XLA Modules:
  0.0 95.8 jit_solution(17129407114107807427)
XLA Ops:
  0.6 91.5 %orthogonalize.1 = (f32[64,2,16,768]{3,2,1,0:T(8,128)S(1)}, bf16[128,16,768]{2,1,0:T(8,128)(2,1)S(1)}, f32[1,2]{1,0:T(1,128)S(1)}) custom-call(bf16[64,2,16,768]{3,2,1,0:T(8,128)(2,1)} %bitcast.6, f32[64,2,16,768]{3,2,1,0:T(8,128)} %bitcast.5, s32[1,128]{1,0:T(1,128)} %bitcast.7), custom_call_target="tpu_custom_call" | custom-call | flops 11000000512 | bytes 18874368 | tf_op jit(solution)/shard_map/orthogonalize/pallas_call | solution.py:366
  92.1 3.7 %store.1 = (f32[128,16,768]{2,1,0:T(8,128)}, bf16[128,16,768]{2,1,0:T(8,128)(2,1)}, f32[1,2]{1,0:T(1,128)}) custom-call(f32[128,16,768]{2,1,0:T(8,128)S(1)} %bitcast.4, bf16[128,16,768]{2,1,0:T(8,128)(2,1)S(1)} %get-tuple-element.7.update_ref, f32[1,2]{1,0:T(1,128)S(1)} %get-tuple-element.8.log_ref), custom_call_target="tpu_custom_call" | custom-call | tf_op jit(solution)/shard_map/store/pallas_call | solution.py:408

commit v7 on v5

--- a/solution.py
+++ b/solution.py
@@ -54,7 +54,7 @@
     barrier = pltpu.get_barrier_semaphore()
 
     def greet(i, carry):
-        t = lax.rem(me + i, DEVICES)
+        t = lax.rem(me + 37 * i, DEVICES)
         pl.semaphore_signal(
             barrier, inc=1, device_id=(lax.div(t, 32), lax.rem(t, 32)), device_id_type=MESH
         )

time: 93.2 us -> 96.3 us (1.033)
  Pallas kernels: 92.3 us -> 95.6 us
    pallas_call x1, Pallas kernels: 88.6 us -> 91.8 us  [on_device(): pl.pallas_call(kernel, out_shape=(jax.ShapeDtypeStruct(paired, F32), jax....]
where the time goes in v7:
time: 96.3 us; the launch traced here: 96.2 us
  Pallas kernels  95.6 us (99%)
    pallas_call x1, Pallas kernels, on_device(): pl.pallas_call(kernel, out_shape=(jax.ShapeDtypeStruct(paired, F32), jax....  91.8 us
    pallas_call x1, Pallas kernels, on_device(): pl.pallas_call(store, out_shape=(jax.ShapeDtypeStruct(momentum.shape, F32...  3.73 us

profile of v7, /device:TPU:1, one launch (start us, length us, event | category | flops | bytes accessed | tf_op | source)
XLA Modules:
  0.0 96.2 jit_solution(16656587349800443371)
XLA Ops:
  0.6 91.8 %orthogonalize.1 = (f32[64,2,16,768]{3,2,1,0:T(8,128)S(1)}, bf16[128,16,768]{2,1,0:T(8,128)(2,1)S(1)}, f32[1,2]{1,0:T(1,128)S(1)}) custom-call(bf16[64,2,16,768]{3,2,1,0:T(8,128)(2,1)} %bitcast.6, f32[64,2,16,768]{3,2,1,0:T(8,128)} %bitcast.5, s32[1,128]{1,0:T(1,128)} %bitcast.7), custom_call_target="tpu_custom_call" | custom-call | flops 11000000512 | bytes 18874368 | tf_op jit(solution)/shard_map/orthogonalize/pallas_call | solution.py:357
  92.5 3.7 %store.1 = (f32[128,16,768]{2,1,0:T(8,128)}, bf16[128,16,768]{2,1,0:T(8,128)(2,1)}, f32[1,2]{1,0:T(1,128)}) custom-call(f32[128,16,768]{2,1,0:T(8,128)S(1)} %bitcast.4, bf16[128,16,768]{2,1,0:T(8,128)(2,1)S(1)} %get-tuple-element.7.update_ref, f32[1,2]{1,0:T(1,128)S(1)} %get-tuple-element.8.log_ref), custom_call_target="tpu_custom_call" | custom-call | tf_op jit(solution)/shard_map/store/pallas_call | solution.py:399
